TPU v7x, 32 devices: a whole 2x2x4 slice. The times are simulated.
32 devices in a mesh: freq: 2 (over x), shot: 8 (over z, y), rcv: 2 (over core).
Axes of the slice: x: 2, y: 2, z: 4, core: 2. Of those that a mesh axis runs over, the one named last changes fastest.
Arguments:
- data_left: float32 [2, 8192, 512], P(None, ('freq', 'shot'), 'rcv'), parts along dimension 1, may hold values from -6 to 6
- slab_table: float32 [2, 2048, 2048], P(None, ('freq', 'shot'), 'rcv'), parts along dimension 1, may hold values from -0.1875 to 0.1875
- recorded: float32 [2, 8192, 2048], P(None, ('freq', 'shot'), 'rcv'), parts along dimension 1, may hold values from -6 to 6
- filter_bank: float32 [16, 17], replicated, may hold values from -1.75 to 1.75
- row_taps: int32 [32], P('shot'), may hold values from 0 to 15
- row_start: int32 [32], P('shot'), may hold values from 0 to 4
- col_taps: int32 [16], P('rcv'), may hold values from 0 to 15
- col_start: int32 [16], P('rcv'), may hold values from 0 to 4
- panel_owner: int32 [8], replicated, may hold values from 0 to 7, each once
- shrink_level: float32 [2048], P('rcv'), may hold values from 0.1 to 0.8
Outputs:
- primaries: float32 [2, 8192, 2048], P(None, ('freq', 'shot'), 'rcv'), parts along dimension 1
There are 2 independent parts, one for each index of `freq`. A program takes and returns all parts, laid end to end along the dimension named above; an argument that names none is the same for every part. Nothing has to cross between parts.
Inputs may be any that keep to these rules, and one draw needn't show every extreme that they name: `panel_owner`: each shot index appears once.
All inputs are finite; a program needn't handle non-finite values.
Results may differ from a plain program's by a relative error of at most 0.0001.
Values sent between devices are 32-bit elements; how exact they have to be, the bound alone decides.
A program may use at most 64 MiB of HBM per device.

v0:
```python
import functools

import jax
import jax.numpy as jnp
from jax import lax
from jax.experimental import pallas as pl
from jax.experimental.pallas import tpu as pltpu
from jax.sharding import PartitionSpec as P

PANEL = 128
PANELS = 4
TAPS = 17
WIN = 13
TBLK = 128
HALO = 8
HOP = 2
SIDE = 2
MESH = pl.DeviceIdType.MESH


def taps_of(bank, index, start, block):
    row, first = index[block], start[block]
    return [
        jnp.where((first <= t) & (t < first + WIN), bank[row, t], jnp.float32(0.0))
        for t in range(TAPS)
    ]


def band_of(taps, distance):
    band = jnp.zeros(distance.shape, jnp.float32)
    for t, weight in enumerate(taps):
        band = jnp.where(distance == t, weight, band)
    return band


def split(x):
    high = x.astype(jnp.bfloat16)
    return high, (x - high.astype(jnp.float32)).astype(jnp.bfloat16)


def kernel(
    n, nr, nlo,
    left, slab, recorded, level, bank, row_taps, row_start, col_taps, col_start, owner,
    out,
    ext, lfilt, lhigh, llow, rec, stage, halo, cut, plane, upin, upout, dnin, dnout, full,
    rec_sem, out_sem, lh_send, lh_recv, sh_send, sh_recv, lf_send, lf_recv,
    cut_send, cut_recv, up_send, up_recv, dn_send, dn_recv, side_send, side_recv,
):
    nhi = n // nlo
    shots, width = left.shape[1], left.shape[2]
    columns = slab.shape[2]
    chunks = columns // TBLK
    items = chunks * PANELS
    piece = PANEL // nlo
    s, r = lax.axis_index("shot"), lax.axis_index("rcv")
    h, l = s // nlo, s % nlo

    def at(shot, rcv):
        return (lax.axis_index("freq"), shot, rcv)

    def remote(src, dst, send, recv, shot, rcv):
        return pltpu.make_async_remote_copy(
            src_ref=src, dst_ref=dst, send_sem=send, recv_sem=recv,
            device_id=at(shot, rcv), device_id_type=MESH,
        )

    barrier = pltpu.get_barrier_semaphore()

    def greet(shot, rcv):
        pl.semaphore_signal(barrier, inc=1, device_id=at(shot, rcv), device_id_type=MESH)

    for k in range(1, nr):
        greet(s, (r + k) % nr)
    for k in range(1, nlo):
        greet(h * nlo + (l + k) % nlo, r)
    pl.when(h > 0)(lambda: greet(s - nlo, r))
    pl.when(h < nhi - 1)(lambda: greet(s + nlo, r))
    pl.when(s > 0)(lambda: greet(s - 1, r))
    pl.when(s < n - 1)(lambda: greet(s + 1, r))
    ends = jnp.int32(nr + nlo - 2)
    for near in (h > 0, h < nhi - 1, s > 0, s < n - 1):
        ends = ends + jnp.where(near, 1, 0)
    pl.semaphore_wait(barrier, ends)

    def slab_halo(to, rcv):
        start = columns - TBLK if to == 0 else 0
        return remote(slab.at[:, :, pl.ds(start, TBLK)], halo.at[to], sh_send.at[to], sh_recv.at[to], s, rcv)

    def left_halo(to, shot):
        start = shots - HALO if to == 0 else 0
        place = 0 if to == 0 else shots + HALO
        return remote(
            left.at[:, pl.ds(start, HALO)], ext.at[:, pl.ds(place, HALO)],
            lh_send.at[to], lh_recv.at[to], shot, r,
        )

    pl.when(r < nr - 1)(lambda: slab_halo(0, r + 1).start())
    pl.when(r > 0)(lambda: slab_halo(1, r - 1).start())
    pl.when(s < n - 1)(lambda: left_halo(0, s + 1).start())
    pl.when(s > 0)(lambda: left_halo(1, s - 1).start())
    fetch = pltpu.make_async_copy(recorded, rec, rec_sem)
    fetch.start()

    @pl.when(r == 0)
    def _():
        halo[0] = jnp.zeros(halo.shape[1:], jnp.float32)

    @pl.when(r == nr - 1)
    def _():
        halo[1] = jnp.zeros(halo.shape[1:], jnp.float32)

    @pl.when(s == 0)
    def _():
        ext[:, :HALO] = jnp.zeros((2, HALO, width), jnp.float32)

    @pl.when(s == n - 1)
    def _():
        ext[:, shots + HALO :] = jnp.zeros((2, HALO, width), jnp.float32)

    ext[:, HALO : shots + HALO] = left[...]
    pl.when(r > 0)(lambda: slab_halo(0, r - 1).wait_recv())
    pl.when(r < nr - 1)(lambda: slab_halo(1, r + 1).wait_recv())

    def lanes(c):
        return pl.ds(pl.multiple_of(c * TBLK, TBLK), TBLK)

    def cut_copy(c, there, sender):
        return remote(
            cut.at[c, there], plane.at[c, sender], cut_send.at[c, there], cut_recv.at[c, sender],
            h * nlo + there, r,
        )

    def filter_slab(c):
        before = jnp.where(c > 0, slab[:, :, lanes(jnp.maximum(c - 1, 0))], halo[0])
        after = jnp.where(c < chunks - 1, slab[:, :, lanes(jnp.minimum(c + 1, chunks - 1))], halo[1])
        whole = jnp.concatenate([before, slab[:, :, lanes(c)], after], axis=2)
        shape = (3 * TBLK, TBLK)
        distance = (
            lax.broadcasted_iota(jnp.int32, shape, 0) - lax.broadcasted_iota(jnp.int32, shape, 1) - (TBLK - HALO)
        )
        band = band_of(taps_of(bank, col_taps, col_start, c), distance)
        done = jnp.dot(
            whole.reshape(2 * PANEL, 3 * TBLK), band,
            preferred_element_type=jnp.float32, precision=lax.Precision.HIGHEST,
        ).reshape(2, PANEL, TBLK)
        for j in range(nlo):
            cut[c, j] = done[:, j * piece : (j + 1) * piece]
        for k in range(1, nlo):
            cut_copy(c, (l + k) % nlo, l).start()
        plane[c, l] = cut[c, l]

    def left_copy(k):
        return remote(lfilt.at[r], lfilt.at[r], lf_send.at[k], lf_recv.at[r], s, (r + k) % nr)

    def left_arrival(k):
        there = (r + k) % nr
        return remote(lfilt.at[there], lfilt.at[there], lf_send.at[k], lf_recv.at[there], s, there)

    def filter_left():
        pl.when(s > 0)(lambda: left_halo(0, s - 1).wait_recv())
        pl.when(s < n - 1)(lambda: left_halo(1, s + 1).wait_recv())
        shape = (TBLK, TBLK + 2 * HALO)
        distance = lax.broadcasted_iota(jnp.int32, shape, 1) - lax.broadcasted_iota(jnp.int32, shape, 0)
        for b in range(shots // TBLK):
            band = band_of(taps_of(bank, row_taps, row_start, b), distance)
            for part in range(2):
                lfilt[r, part, b * TBLK : (b + 1) * TBLK] = jnp.dot(
                    band, ext[part, b * TBLK : b * TBLK + TBLK + 2 * HALO],
                    preferred_element_type=jnp.float32, precision=lax.Precision.HIGHEST,
                )
        for k in range(1, nr):
            left_copy(k).start()

    def join_left():
        for k in range(1, nr):
            left_arrival(k).wait_recv()
        for j in range(nr):
            high, low = split(lfilt[j])
            lhigh[:, :, j * width : (j + 1) * width] = high
            llow[:, :, j * width : (j + 1) * width] = low

    def up_copy(c, p, shot):
        return remote(upout.at[c, p], upin.at[c, p], up_send.at[c], up_recv.at[c * PANELS + p], shot, r)

    def dn_copy(c, p, shot):
        return remote(dnout.at[c, p], dnin.at[c, p], dn_send.at[c], dn_recv.at[c * PANELS + p], shot, r)

    def mine(c, p):
        place = owner[p] % nlo
        value = plane[c, 0]
        for j in range(1, nlo):
            value = jnp.where(place == j, plane[c, j], value)
        return value

    def side_copy(c, p, there):
        return remote(
            full.at[c, l, p], full.at[c, l, p], side_send.at[c, there], side_recv.at[c, l], h * nlo + there, r
        )

    def side_whole(c, sender, there):
        return remote(
            full.at[c, sender], full.at[c, sender], side_send.at[c, there], side_recv.at[c, sender],
            h * nlo + there, r,
        )

    def move_up(c, p):
        @pl.when(h == 0)
        def _():
            upin[c, p] = jnp.zeros(upin.shape[2:], jnp.float32)

        @pl.when(h > 0)
        def _():
            up_copy(c, p, s - nlo).wait_recv()

        @pl.when(h < nhi - 1)
        def _():
            upout[c, p] = jnp.where(owner[p] // nlo == h, mine(c, p), upin[c, p])
            up_copy(c, p, s + nlo).start()

    def move_down(c, p):
        @pl.when(h == nhi - 1)
        def _():
            dnin[c, p] = jnp.zeros(dnin.shape[2:], jnp.float32)

        @pl.when(h < nhi - 1)
        def _():
            dn_copy(c, p, s + nlo).wait_recv()

        @pl.when(h > 0)
        def _():
            dnout[c, p] = jnp.where(owner[p] // nlo == h, mine(c, p), dnin[c, p])
            dn_copy(c, p, s - nlo).start()

    def settle(c, p):
        line = owner[p] // nlo
        value = jnp.where(line < h, upin[c, p], dnin[c, p])
        full[c, l, p] = jnp.where(line == h, mine(c, p), value)
        for k in range(1, nlo):
            side_copy(c, p, (l + k) % nlo).start()

    def out_copy(c):
        return pltpu.make_async_copy(stage.at[c], out.at[:, :, lanes(c)], out_sem.at[c])

    def product(c):
        for k in range(1, nlo):
            side_whole(c, (l + k) % nlo, l).wait_recv()
        pl.when(c == 0)(join_left)
        pl.when(c == 0)(fetch.wait)
        right = jnp.concatenate(
            [
                jnp.concatenate([full[c, j, p, part] for p in range(PANELS) for j in range(nlo)], axis=0)
                for part in range(2)
            ],
            axis=1,
        )
        high, low = split(right)

        def times(part, rows):
            a, b = lhigh[part, rows], llow[part, rows]
            dot = functools.partial(jnp.dot, preferred_element_type=jnp.float32)
            return dot(a, high) + (dot(a, low) + dot(b, high))

        threshold = level[:, lanes(c)]
        for b in range(shots // (2 * TBLK)):
            rows = slice(b * 2 * TBLK, (b + 1) * 2 * TBLK)
            x, y = times(0, rows), times(1, rows)
            real = rec[0, rows, lanes(c)] - (x[:, :TBLK] - y[:, TBLK:])
            imag = rec[1, rows, lanes(c)] - (x[:, TBLK:] + y[:, :TBLK])
            magnitude = jnp.sqrt(real * real + imag * imag)
            factor = jnp.maximum(magnitude - threshold, 0.0) / jnp.maximum(magnitude, threshold)
            stage[c, 0, rows] = real * factor
            stage[c, 1, rows] = imag * factor
        out_copy(c).start()

    last = HOP * (nhi - 1)
    filter_slab(0)

    def step(k, carry):
        @pl.when((k % PANELS == 0) & (k // PANELS < chunks - 1))
        def _():
            filter_slab(k // PANELS + 1)

        @pl.when((k % PANELS == 0) & (k < items))
        def _():
            for j in range(1, nlo):
                cut_copy(k // PANELS, l, (l + j) % nlo).wait_recv()

        i = k - HOP * h

        @pl.when((i >= 0) & (i < items))
        def _():
            move_up(i // PANELS, i % PANELS)

        j = k - HOP * (nhi - 1 - h)

        @pl.when((j >= 0) & (j < items))
        def _():
            move_down(j // PANELS, j % PANELS)

        m = k - last

        @pl.when((m >= 0) & (m < items))
        def _():
            settle(m // PANELS, m % PANELS)

        q = k - last - SIDE - (PANELS - 1)

        pl.when(k == 1)(filter_left)

        @pl.when((q >= 0) & (q % PANELS == 0))
        def _():
            product(q // PANELS)

        return carry

    lax.fori_loop(0, items + last + SIDE, step, 0)

    pl.when(r < nr - 1)(lambda: slab_halo(0, r + 1).wait_send())
    pl.when(r > 0)(lambda: slab_halo(1, r - 1).wait_send())
    pl.when(s < n - 1)(lambda: left_halo(0, s + 1).wait_send())
    pl.when(s > 0)(lambda: left_halo(1, s - 1).wait_send())
    for k in range(1, nr):
        left_copy(k).wait_send()

    def drain(c, carry):
        for k in range(1, nlo):
            there = (l + k) % nlo
            cut_copy(c, there, l).wait_send()
            side_whole(c, l, there).wait_send()

        @pl.when(h < nhi - 1)
        def _():
            remote(upout.at[c], upin.at[c], up_send.at[c], up_recv.at[0], s + nlo, r).wait_send()

        @pl.when(h > 0)
        def _():
            remote(dnout.at[c], dnin.at[c], dn_send.at[c], dn_recv.at[0], s - nlo, r).wait_send()

        out_copy(c).wait()
        return carry

    lax.fori_loop(0, chunks, drain, 0)


def body(n, nr, data_left, slab_table, recorded, bank, row_taps, row_start, col_taps, col_start, owner, level):
    nlo = 1
    while (2 * nlo) ** 2 <= n and n % (2 * nlo) == 0:
        nlo *= 2
    shots, width = data_left.shape[1], data_left.shape[2]
    columns = slab_table.shape[2]
    chunks = columns // TBLK
    piece = PANEL // nlo
    items = chunks * PANELS
    vmem, smem = pl.BlockSpec(memory_space=pltpu.VMEM), pl.BlockSpec(memory_space=pltpu.SMEM)
    hbm = pl.BlockSpec(memory_space=pl.ANY)
    f32 = jnp.float32
    dma = pltpu.SemaphoreType.DMA
    flow = pltpu.VMEM((chunks, PANELS, 2, piece, TBLK), f32)
    return pl.pallas_call(
        functools.partial(kernel, n, nr, nlo),
        out_shape=jax.ShapeDtypeStruct(recorded.shape, f32),
        in_specs=[vmem, vmem, hbm, vmem] + [smem] * 6,
        out_specs=hbm,
        scratch_shapes=[
            pltpu.VMEM((2, shots + 2 * HALO, width), f32),
            pltpu.VMEM((nr, 2, shots, width), f32),
            pltpu.VMEM((2, shots, nr * width), jnp.bfloat16),
            pltpu.VMEM((2, shots, nr * width), jnp.bfloat16),
            pltpu.VMEM((2, shots, columns), f32),
            pltpu.VMEM((chunks, 2, shots, TBLK), f32),
            pltpu.VMEM((2, 2, PANEL, TBLK), f32),
            pltpu.VMEM((chunks, nlo, 2, piece, TBLK), f32),
            pltpu.VMEM((chunks, nlo, 2, piece, TBLK), f32),
            flow, flow, flow, flow,
            pltpu.VMEM((chunks, nlo, PANELS, 2, piece, TBLK), f32),
            dma, dma((chunks,)), dma((2,)), dma((2,)), dma((2,)), dma((2,)), dma((nr,)), dma((nr,)),
            dma((chunks, nlo)), dma((chunks, nlo)), dma((chunks,)), dma((items,)), dma((chunks,)), dma((items,)),
            dma((chunks, nlo)), dma((chunks, nlo)),
        ],
        compiler_params=pltpu.CompilerParams(
            collective_id=0, has_side_effects=True, vmem_limit_bytes=56 * 2**20
        ),
    )(data_left, slab_table, recorded, level.reshape(1, columns), bank, row_taps, row_start, col_taps, col_start, owner)


def solution(mesh):
    block = P(None, ("freq", "shot"), "rcv")
    return jax.shard_map(
        functools.partial(body, mesh.shape["shot"], mesh.shape["rcv"]),
        mesh=mesh,
        in_specs=(block, block, block, P(), P("shot"), P("shot"), P("rcv"), P("rcv"), P(), P("rcv")),
        out_specs=block,
        check_vma=False,
    )
```

profile of v0, /device:TPU:0, one launch (start us, length us, event | category | flops | bytes accessed | tf_op | source)
XLA Modules:
  0.0 87.6 jit_solution(6809774373053361458)
XLA Ops:
  0.0 82.8 %shard_map.100 = f32[2,512,1024]{2,1,0:T(8,128)} custom-call(f32[2,512,256]{2,1,0:T(8,128)} %left.1, f32[2,128,1024]{2,1,0:T(8,128)} %slab.1, f32[2,512,1024]{2,1,0:T(8,128)} %recorded.1, f32[1,1024]{1,0:T(1,128)} %bitcast.1, f32[16,17]{1,0:T(8,128)} %bank.1, s32[4]{0:T(128)} %row_taps.1, s32[4]{0:T(128)} %row_start.1, s32[8]{0:T(128)} %col_taps.1, ...), custom_call_target="tpu_custom_call" | custom-call | tf_op jit(solution)/shard_map/pallas_call | solution.py:359
  82.8 4.8 %copy.12 = f32[2,512,1024]{2,1,0:T(8,128)} copy(f32[2,512,1024]{2,1,0:T(8,128)} %shard_map.100) | data formatting | bytes 8388608
where the time goes:
time: 87.8 us; the launch traced here: 87.6 us
  Pallas kernels  82.8 us (94%)
  local copies, waits for them, and re-layouts  4.79 us (5%)
    pallas_call x1, Pallas kernels, body(): pl.pallas_call(functools.partial(kernel, n, nr, nlo), out_shape=jax.Shape...  82.8 us
    unnamed x1, local copies, waits for them, and re-layouts  4.79 us

commit v1 on v0

--- a/solution.py
+++ b/solution.py
@@ -13,8 +13,10 @@
 WIN = 13
 TBLK = 128
 HALO = 8
-HOP = 2
-SIDE = 2
+HOP = 6
+SIDE = 4
+PARTS = 2
+ROUND = PANELS * PARTS
 MESH = pl.DeviceIdType.MESH
 
 
@@ -50,7 +52,7 @@
     shots, width = left.shape[1], left.shape[2]
     columns = slab.shape[2]
     chunks = columns // TBLK
-    items = chunks * PANELS
+    items = chunks * ROUND
     piece = PANEL // nlo
     s, r = lax.axis_index("shot"), lax.axis_index("rcv")
     h, l = s // nlo, s % nlo
@@ -179,22 +181,28 @@
             lhigh[:, :, j * width : (j + 1) * width] = high
             llow[:, :, j * width : (j + 1) * width] = low
 
-    def up_copy(c, p, shot):
-        return remote(upout.at[c, p], upin.at[c, p], up_send.at[c], up_recv.at[c * PANELS + p], shot, r)
-
-    def dn_copy(c, p, shot):
-        return remote(dnout.at[c, p], dnin.at[c, p], dn_send.at[c], dn_recv.at[c * PANELS + p], shot, r)
-
-    def mine(c, p):
+    def up_copy(c, p, part, shot):
+        return remote(
+            upout.at[c, p, part], upin.at[c, p, part], up_send.at[c],
+            up_recv.at[c * ROUND + p * PARTS + part], shot, r,
+        )
+
+    def dn_copy(c, p, part, shot):
+        return remote(
+            dnout.at[c, p, part], dnin.at[c, p, part], dn_send.at[c],
+            dn_recv.at[c * ROUND + p * PARTS + part], shot, r,
+        )
+
+    def mine(c, p, part):
         place = owner[p] % nlo
-        value = plane[c, 0]
+        value = plane[c, 0, part]
         for j in range(1, nlo):
-            value = jnp.where(place == j, plane[c, j], value)
+            value = jnp.where(place == j, plane[c, j, part], value)
         return value
 
-    def side_copy(c, p, there):
-        return remote(
-            full.at[c, l, p], full.at[c, l, p], side_send.at[c, there], side_recv.at[c, l], h * nlo + there, r
+    def side_copy(c, p, part, there):
+        return remote(
+            full.at[c, l, p, part], full.at[c, l, p, part], side_send.at[c, there], side_recv.at[c, l], h * nlo + there, r
         )
 
     def side_whole(c, sender, there):
@@ -203,40 +211,40 @@
             h * nlo + there, r,
         )
 
-    def move_up(c, p):
+    def move_up(c, p, part):
         @pl.when(h == 0)
         def _():
-            upin[c, p] = jnp.zeros(upin.shape[2:], jnp.float32)
+            upin[c, p, part] = jnp.zeros(upin.shape[3:], jnp.float32)
 
         @pl.when(h > 0)
         def _():
-            up_copy(c, p, s - nlo).wait_recv()
+            up_copy(c, p, part, s - nlo).wait_recv()
 
         @pl.when(h < nhi - 1)
         def _():
-            upout[c, p] = jnp.where(owner[p] // nlo == h, mine(c, p), upin[c, p])
-            up_copy(c, p, s + nlo).start()
-
-    def move_down(c, p):
+            upout[c, p, part] = jnp.where(owner[p] // nlo == h, mine(c, p, part), upin[c, p, part])
+            up_copy(c, p, part, s + nlo).start()
+
+    def move_down(c, p, part):
         @pl.when(h == nhi - 1)
         def _():
-            dnin[c, p] = jnp.zeros(dnin.shape[2:], jnp.float32)
+            dnin[c, p, part] = jnp.zeros(dnin.shape[3:], jnp.float32)
 
         @pl.when(h < nhi - 1)
         def _():
-            dn_copy(c, p, s + nlo).wait_recv()
+            dn_copy(c, p, part, s + nlo).wait_recv()
 
         @pl.when(h > 0)
         def _():
-            dnout[c, p] = jnp.where(owner[p] // nlo == h, mine(c, p), dnin[c, p])
-            dn_copy(c, p, s - nlo).start()
-
-    def settle(c, p):
+            dnout[c, p, part] = jnp.where(owner[p] // nlo == h, mine(c, p, part), dnin[c, p, part])
+            dn_copy(c, p, part, s - nlo).start()
+
+    def settle(c, p, part):
         line = owner[p] // nlo
-        value = jnp.where(line < h, upin[c, p], dnin[c, p])
-        full[c, l, p] = jnp.where(line == h, mine(c, p), value)
+        value = jnp.where(line < h, upin[c, p, part], dnin[c, p, part])
+        full[c, l, p, part] = jnp.where(line == h, mine(c, p, part), value)
         for k in range(1, nlo):
-            side_copy(c, p, (l + k) % nlo).start()
+            side_copy(c, p, part, (l + k) % nlo).start()
 
     def out_copy(c):
         return pltpu.make_async_copy(stage.at[c], out.at[:, :, lanes(c)], out_sem.at[c])
@@ -276,40 +284,40 @@
     filter_slab(0)
 
     def step(k, carry):
-        @pl.when((k % PANELS == 0) & (k // PANELS < chunks - 1))
-        def _():
-            filter_slab(k // PANELS + 1)
-
-        @pl.when((k % PANELS == 0) & (k < items))
+        @pl.when(k < chunks - 1)
+        def _():
+            filter_slab(k + 1)
+
+        pl.when(k == 0)(filter_left)
+
+        @pl.when((k % ROUND == 0) & (k < items))
         def _():
             for j in range(1, nlo):
-                cut_copy(k // PANELS, l, (l + j) % nlo).wait_recv()
+                cut_copy(k // ROUND, l, (l + j) % nlo).wait_recv()
 
         i = k - HOP * h
 
         @pl.when((i >= 0) & (i < items))
         def _():
-            move_up(i // PANELS, i % PANELS)
+            move_up(i // ROUND, i // PARTS % PANELS, i % PARTS)
 
         j = k - HOP * (nhi - 1 - h)
 
         @pl.when((j >= 0) & (j < items))
         def _():
-            move_down(j // PANELS, j % PANELS)
+            move_down(j // ROUND, j // PARTS % PANELS, j % PARTS)
 
         m = k - last
 
         @pl.when((m >= 0) & (m < items))
         def _():
-            settle(m // PANELS, m % PANELS)
-
-        q = k - last - SIDE - (PANELS - 1)
-
-        pl.when(k == 1)(filter_left)
-
-        @pl.when((q >= 0) & (q % PANELS == 0))
-        def _():
-            product(q // PANELS)
+            settle(m // ROUND, m // PARTS % PANELS, m % PARTS)
+
+        q = k - last - SIDE - (ROUND - 1)
+
+        @pl.when((q >= 0) & (q % ROUND == 0))
+        def _():
+            product(q // ROUND)
 
         return carry
 
@@ -350,7 +358,7 @@
     columns = slab_table.shape[2]
     chunks = columns // TBLK
     piece = PANEL // nlo
-    items = chunks * PANELS
+    items = chunks * ROUND
     vmem, smem = pl.BlockSpec(memory_space=pltpu.VMEM), pl.BlockSpec(memory_space=pltpu.SMEM)
     hbm = pl.BlockSpec(memory_space=pl.ANY)
     f32 = jnp.float32

time: 87.8 us -> 79.8 us (0.909)
  Pallas kernels: 82.8 us -> 74.8 us
    pallas_call x1, Pallas kernels: 82.8 us -> 74.8 us  [body(): pl.pallas_call(functools.partial(kernel, n, nr, nlo), out_shape=jax.Shape...]
where the time goes in v1:
time: 79.8 us; the launch traced here: 79.6 us
  Pallas kernels  74.8 us (94%)
  local copies, waits for them, and re-layouts  4.79 us (6%)
    pallas_call x1, Pallas kernels, body(): pl.pallas_call(functools.partial(kernel, n, nr, nlo), out_shape=jax.Shape...  74.8 us
    unnamed x1, local copies, waits for them, and re-layouts  4.79 us

profile of v1, /device:TPU:0, one launch (start us, length us, event | category | flops | bytes accessed | tf_op | source)
XLA Modules:
  0.0 79.6 jit_solution(8360439748509189008)
XLA Ops:
  0.0 74.8 %shard_map.100 = f32[2,512,1024]{2,1,0:T(8,128)} custom-call(f32[2,512,256]{2,1,0:T(8,128)} %left.1, f32[2,128,1024]{2,1,0:T(8,128)} %slab.1, f32[2,512,1024]{2,1,0:T(8,128)} %recorded.1, f32[1,1024]{1,0:T(1,128)} %bitcast.1, f32[16,17]{1,0:T(8,128)} %bank.1, s32[4]{0:T(128)} %row_taps.1, s32[4]{0:T(128)} %row_start.1, s32[8]{0:T(128)} %col_taps.1, ...), custom_call_target="tpu_custom_call" | custom-call | tf_op jit(solution)/shard_map/pallas_call | solution.py:367
  74.8 4.8 %copy.12 = f32[2,512,1024]{2,1,0:T(8,128)} copy(f32[2,512,1024]{2,1,0:T(8,128)} %shard_map.100) | data formatting | bytes 8388608

commit v2 on v1

--- a/solution.py
+++ b/solution.py
@@ -14,7 +14,7 @@
 TBLK = 128
 HALO = 8
 HOP = 6
-SIDE = 4
+SIDE = 8
 PARTS = 2
 ROUND = PANELS * PARTS
 MESH = pl.DeviceIdType.MESH
@@ -307,7 +307,7 @@
         def _():
             move_down(j // ROUND, j // PARTS % PANELS, j % PARTS)
 
-        m = k - last
+        m = k - HOP * jnp.maximum(h, nhi - 1 - h)
 
         @pl.when((m >= 0) & (m < items))
         def _():

time: 79.8 us -> 77.3 us (0.969)
  Pallas kernels: 74.8 us -> 72.3 us
    pallas_call x1, Pallas kernels: 74.8 us -> 72.3 us  [body(): pl.pallas_call(functools.partial(kernel, n, nr, nlo), out_shape=jax.Shape...]
where the time goes in v2:
time: 77.3 us; the launch traced here: 77.1 us
  Pallas kernels  72.3 us (94%)
  local copies, waits for them, and re-layouts  4.79 us (6%)
    pallas_call x1, Pallas kernels, body(): pl.pallas_call(functools.partial(kernel, n, nr, nlo), out_shape=jax.Shape...  72.3 us
    unnamed x1, local copies, waits for them, and re-layouts  4.79 us

profile of v2, /device:TPU:0, one launch (start us, length us, event | category | flops | bytes accessed | tf_op | source)
XLA Modules:
  0.0 77.1 jit_solution(5944700195638221537)
XLA Ops:
  0.0 72.3 %shard_map.100 = f32[2,512,1024]{2,1,0:T(8,128)} custom-call(f32[2,512,256]{2,1,0:T(8,128)} %left.1, f32[2,128,1024]{2,1,0:T(8,128)} %slab.1, f32[2,512,1024]{2,1,0:T(8,128)} %recorded.1, f32[1,1024]{1,0:T(1,128)} %bitcast.1, f32[16,17]{1,0:T(8,128)} %bank.1, s32[4]{0:T(128)} %row_taps.1, s32[4]{0:T(128)} %row_start.1, s32[8]{0:T(128)} %col_taps.1, ...), custom_call_target="tpu_custom_call" | custom-call | tf_op jit(solution)/shard_map/pallas_call | solution.py:367
  72.3 4.8 %copy.12 = f32[2,512,1024]{2,1,0:T(8,128)} copy(f32[2,512,1024]{2,1,0:T(8,128)} %shard_map.100) | data formatting | bytes 8388608
